TPU v7x, 512 devices: a whole 4x4x16 slice. The times are simulated.
512 devices in a mesh: seq: 32 (over x, z_lo, core), head: 16 (over y, z_hi).
Axes of the slice: x: 4, y: 4, z: 16 (z_hi: 4, z_lo: 4; z = z_hi * 4 + z_lo), core: 2. Of those that a mesh axis runs over, the one named last changes fastest.
Arguments:
- out_grad: bfloat16 [8192, 4096], P('seq', 'head'), may hold values from -7.2 to 7.2
- x_in: bfloat16 [8192, 4096], P('seq', 'head'), may hold values from -6 to 6
- b_in: bfloat16 [8192, 128], P('seq'), may hold values from -2.5 to 2.5
- c_in: bfloat16 [8192, 128], P('seq'), may hold values from -2.5 to 2.5
- dt_raw: float32 [64, 8192], P('head', 'seq'), may hold values from -5.1 to -0.7
- dt_bias: float32 [64], P('head'), may hold values from -0.5 to 0.5
- a_log: float32 [64], P('head'), may hold values from -7.5 to 2.2
- d_skip: float32 [64], P('head'), may hold values from 0.5 to 1.5
- states: bfloat16 [32, 4096, 128], P('seq', 'head'), may hold values from -6 to 6
- w_out: bfloat16 [4096, 4096], P('head'), may hold values from -0.09375 to 0.09375
- w_in: bfloat16 [4096, 4096], P(None, 'head'), may hold values from -0.125 to 0.125
Outputs:
- in_grad: bfloat16 [4096, 8192], P('head', 'seq')
- bc_grad: bfloat16 [256, 8192], P('head', 'seq')
- dt_grad: float32 [64, 8192], P('head', 'seq')
- param_grad: float32 [3, 64], P(None, 'head')
All inputs are finite; a program needn't handle non-finite values.
Results may differ from a plain program's by a relative error of at most 0.015.
Values may be sent and summed in bfloat16 or wider, within the bound.
No kernel may reach another device: no remote copies, remote signals or barrier semaphores. Data moves between devices by JAX's collectives and lax.ppermute only.
A program may use at most 64 MiB of HBM per device.

v0:
```python
import jax
import jax.numpy as jnp
from jax import lax
from jax.sharding import PartitionSpec as P


def passed_along(value, axis, steps):
    count = lax.axis_size(axis)
    initial, last = (max(0, -steps), min(count, count - steps))
    return lax.ppermute(value, axis, [(source, source + steps) for source in range(initial, last)])


def shards(out_grad, x_in, b_in, c_in, dt_raw, dt_bias, a_log, d_skip, states, w_out, w_in):
    tokens_here, inner_here = x_in.shape
    group_heads = dt_raw.shape[0]
    head_dim = inner_here // group_heads
    state_dim = b_in.shape[1]
    contract_last = (((1,), (1,)), ((), ()))
    head_sum = lax.dot_general(
        lax.all_gather(out_grad, "head", axis=1, tiled=True),
        w_out,
        contract_last,
        preferred_element_type=jnp.float32,
    )
    dy_heads = head_sum.astype(jnp.bfloat16).reshape(tokens_here, group_heads, head_dim)
    dy_wide = dy_heads.astype(jnp.float32)
    x_heads = x_in.reshape(tokens_here, group_heads, head_dim)
    x_wide = x_heads.astype(jnp.float32)
    decay_rate = jnp.exp(a_log)
    step_size = jax.nn.softplus(dt_raw + dt_bias[:, None])
    log_step = -decay_rate[:, None] * step_size
    cumlog = jnp.cumsum(log_step, axis=1)
    positions = jnp.arange(tokens_here)
    causal = positions[:, None] >= positions[None, :]
    log_gaps = cumlog[:, :, None] - cumlog[:, None, :]
    decay_mask = jnp.where(causal[None], jnp.exp(jnp.minimum(log_gaps, 0.0)), 0.0)
    scores = lax.dot_general(c_in, b_in, contract_last, preferred_element_type=jnp.float32)
    step_rows = step_size.T
    x_scaled = (x_wide * step_rows[:, :, None]).astype(jnp.bfloat16)
    pair_dots = jnp.einsum("ihp,jhp->hij", dy_heads, x_scaled, preferred_element_type=jnp.float32)
    kernel = (scores[None] * decay_mask).astype(jnp.bfloat16)
    intra_back = jnp.einsum("hij,ihp->jhp", kernel, dy_heads, preferred_element_type=jnp.float32)
    masked_dots = (pair_dots * decay_mask).astype(jnp.bfloat16)
    start_decay = jnp.exp(cumlog)
    dy_decay = (dy_wide * start_decay.T[:, :, None]).astype(jnp.bfloat16)
    local_state = jnp.einsum("ihp,in->hpn", dy_decay, c_in, preferred_element_type=jnp.float32)
    end_total = jnp.exp(cumlog[:, -1])
    entry_state = states.reshape(group_heads, head_dim, state_dim)
    db_intra = jnp.einsum("hij,in->nj", masked_dots, c_in, preferred_element_type=jnp.float32)
    dc_intra = jnp.einsum("hij,jn->ni", masked_dots, b_in, preferred_element_type=jnp.float32)
    dc_entry = jnp.einsum("ihp,hpn->ni", dy_decay, entry_state, preferred_element_type=jnp.float32)
    ystate = jnp.einsum("in,hpn->ihp", c_in, entry_state, preferred_element_type=jnp.float32)
    pair_weight = pair_dots * scores[None] * decay_mask
    state_terms = start_decay * jnp.sum(dy_wide * ystate, axis=2).T
    skip_terms = jnp.sum(dy_wide * x_wide, axis=(0, 2))

    def relay_turn(turn_index, held_state):
        return passed_along(end_total[:, None, None] * held_state + local_state, "seq", -1)

    carried = lax.fori_loop(0, lax.axis_size("seq") - 1, relay_turn, jnp.zeros_like(local_state))
    carried_bf = carried.astype(jnp.bfloat16)
    state_back = jnp.einsum("jn,hpn->jhp", b_in, carried_bf, preferred_element_type=jnp.float32)
    end_decay = jnp.exp(cumlog[:, -1:] - cumlog)
    end_weight = (step_size * end_decay).T
    x_grad = (
        (
            step_rows[:, :, None] * intra_back
            + end_weight[:, :, None] * state_back
            + d_skip[None, :, None] * dy_wide
        )
        .astype(jnp.bfloat16)
        .reshape(tokens_here, inner_here)
    )
    x_end = (x_wide * end_weight[:, :, None]).astype(jnp.bfloat16)
    db_entry = jnp.einsum("jhp,hpn->nj", x_end, carried_bf, preferred_element_type=jnp.float32)
    bc_part = jnp.concatenate([db_intra + db_entry, dc_intra + dc_entry], axis=0)
    end_terms = end_weight.T * jnp.sum(x_wide * state_back, axis=2).T
    cum_grad = pair_weight.sum(axis=2) - pair_weight.sum(axis=1) + state_terms - end_terms
    tail_grad = end_terms.sum(axis=1) + end_total * jnp.sum(
        entry_state.astype(jnp.float32) * carried, axis=(1, 2)
    )
    cum_grad = cum_grad.at[:, -1].add(tail_grad)
    step_grad = jnp.cumsum(cum_grad[:, ::-1], axis=1)[:, ::-1]
    dt_sum = (
        -decay_rate[:, None] * step_grad
        + jnp.sum(x_wide * (intra_back + end_decay.T[:, :, None] * state_back), axis=2).T
    )
    dt_grad = dt_sum * jax.nn.sigmoid(dt_raw + dt_bias[:, None])
    param_terms = jnp.stack(
        [jnp.sum(step_grad * log_step, axis=1), skip_terms, jnp.sum(dt_grad, axis=1)]
    )
    in_part = lax.psum_scatter(
        lax.dot_general(w_in, x_grad, contract_last, preferred_element_type=jnp.float32).astype(
            jnp.bfloat16
        ),
        "head",
        scatter_dimension=0,
        tiled=True,
    )
    bc_sum = lax.psum_scatter(bc_part.astype(jnp.bfloat16), "head", scatter_dimension=0, tiled=True)
    norm_scale = (lax.axis_size("seq") * tokens_here * head_dim) ** (-0.5)
    param_grad = lax.psum(param_terms, "seq") * norm_scale
    return (in_part, bc_sum, dt_grad, param_grad)


def solution(mesh):
    return jax.shard_map(
        shards,
        mesh=mesh,
        in_specs=(
            P("seq", "head"),
            P("seq", "head"),
            P("seq", None),
            P("seq", None),
            P("head", "seq"),
            P("head"),
            P("head"),
            P("head"),
            P("seq", "head", None),
            P("head", None),
            P(None, "head"),
        ),
        out_specs=(P("head", "seq"), P("head", "seq"), P("head", "seq"), P(None, "head")),
        check_vma=False,
    )
```

profile of v0, /device:TPU:2, one launch (start us, length us, event | category | flops | bytes accessed | tf_op | source)
XLA Modules:
  0.0 642.7 jit_solution(2640681701304499436)
XLA Ops:
  14.1 103.5 %all-gather.2.cloned.1.call-done = bf16[256,4096]{1,0:T(8,128)(2,1)} async-done(((bf16[256,256]{1,0:T(8,128)(2,1)}), bf16[256,4096]{1,0:T(8,128)(2,1)}) %all-gather.2.cloned.1.call-update) | async-done | bytes 2097168 | tf_op jit(solution)/shard_map/all_gather | solution.py:20
  117.7 3.1 fusion.14
  122.1 276.6 %while.11 = (s32[]{:T(128)}, f32[4,64,128]{2,1,0:T(8,128)S(1)}, f32[4]{0:T(128)S(1)}, f32[4,64,128]{2,1,0:T(8,128)S(1)}, s32[]{:T(128)}) while((s32[]{:T(128)}, f32[4,64,128]{2,1,0:T(8,128)S(1)}, f32[4]{0:T(128)S(1)}, f32[4,64,128]{2,1,0:T(8,128)S(1)}, s32[]{:T(128)}) %tuple.42), condition=%wide.region_3.4_spmd, body=%wide.region_2.3_spmd.sunk | while | flops 65538 | bytes 917621 | solution.py:60
  126.7 6.5 %collective-permute-start = (f32[4,64,128]{2,1,0:T(8,128)S(1)}, f32[4,64,128]{2,1,0:T(8,128)S(1)}, u32[]{:S(2)}, u32[]{:S(2)}) collective-permute-start(f32[4,64,128]{2,1,0:T(8,128)S(1)} %multiply_add_fusion.2), channel_id=1, source_target_pairs={{16,0},{32,16},{48,32},{64,48},{80,64},{96,80},{112,96},{128,112},... | collective-permute-start | bytes 393224 | tf_op jit(solution)/shard_map/while/body/eval_jaxpr/ppermute | solution.py:10
  135.8 6.5 %collective-permute-start = (f32[4,64,128]{2,1,0:T(8,128)S(1)}, f32[4,64,128]{2,1,0:T(8,128)S(1)}, u32[]{:S(2)}, u32[]{:S(2)}) collective-permute-start(f32[4,64,128]{2,1,0:T(8,128)S(1)} %multiply_add_fusion.2), channel_id=1, source_target_pairs={{16,0},{32,16},{48,32},{64,48},{80,64},{96,80},{112,96},{128,112},... | collective-permute-start | bytes 393224 | tf_op jit(solution)/shard_map/while/body/eval_jaxpr/ppermute | solution.py:10
  142.3 2.5 collective-permute-done
  144.9 6.5 %collective-permute-start = (f32[4,64,128]{2,1,0:T(8,128)S(1)}, f32[4,64,128]{2,1,0:T(8,128)S(1)}, u32[]{:S(2)}, u32[]{:S(2)}) collective-permute-start(f32[4,64,128]{2,1,0:T(8,128)S(1)} %multiply_add_fusion.2), channel_id=1, source_target_pairs={{16,0},{32,16},{48,32},{64,48},{80,64},{96,80},{112,96},{128,112},... | collective-permute-start | bytes 393224 | tf_op jit(solution)/shard_map/while/body/eval_jaxpr/ppermute | solution.py:10
  151.4 2.5 collective-permute-done
  153.9 6.5 %collective-permute-start = (f32[4,64,128]{2,1,0:T(8,128)S(1)}, f32[4,64,128]{2,1,0:T(8,128)S(1)}, u32[]{:S(2)}, u32[]{:S(2)}) collective-permute-start(f32[4,64,128]{2,1,0:T(8,128)S(1)} %multiply_add_fusion.2), channel_id=1, source_target_pairs={{16,0},{32,16},{48,32},{64,48},{80,64},{96,80},{112,96},{128,112},... | collective-permute-start | bytes 393224 | tf_op jit(solution)/shard_map/while/body/eval_jaxpr/ppermute | solution.py:10
  163.0 6.5 %collective-permute-start = (f32[4,64,128]{2,1,0:T(8,128)S(1)}, f32[4,64,128]{2,1,0:T(8,128)S(1)}, u32[]{:S(2)}, u32[]{:S(2)}) collective-permute-start(f32[4,64,128]{2,1,0:T(8,128)S(1)} %multiply_add_fusion.2), channel_id=1, source_target_pairs={{16,0},{32,16},{48,32},{64,48},{80,64},{96,80},{112,96},{128,112},... | collective-permute-start | bytes 393224 | tf_op jit(solution)/shard_map/while/body/eval_jaxpr/ppermute | solution.py:10
  172.1 6.5 %collective-permute-start = (f32[4,64,128]{2,1,0:T(8,128)S(1)}, f32[4,64,128]{2,1,0:T(8,128)S(1)}, u32[]{:S(2)}, u32[]{:S(2)}) collective-permute-start(f32[4,64,128]{2,1,0:T(8,128)S(1)} %multiply_add_fusion.2), channel_id=1, source_target_pairs={{16,0},{32,16},{48,32},{64,48},{80,64},{96,80},{112,96},{128,112},... | collective-permute-start | bytes 393224 | tf_op jit(solution)/shard_map/while/body/eval_jaxpr/ppermute | solution.py:10
  178.6 2.5 collective-permute-done
  181.1 6.5 %collective-permute-start = (f32[4,64,128]{2,1,0:T(8,128)S(1)}, f32[4,64,128]{2,1,0:T(8,128)S(1)}, u32[]{:S(2)}, u32[]{:S(2)}) collective-permute-start(f32[4,64,128]{2,1,0:T(8,128)S(1)} %multiply_add_fusion.2), channel_id=1, source_target_pairs={{16,0},{32,16},{48,32},{64,48},{80,64},{96,80},{112,96},{128,112},... | collective-permute-start | bytes 393224 | tf_op jit(solution)/shard_map/while/body/eval_jaxpr/ppermute | solution.py:10
  187.6 2.5 collective-permute-done
  190.2 6.5 %collective-permute-start = (f32[4,64,128]{2,1,0:T(8,128)S(1)}, f32[4,64,128]{2,1,0:T(8,128)S(1)}, u32[]{:S(2)}, u32[]{:S(2)}) collective-permute-start(f32[4,64,128]{2,1,0:T(8,128)S(1)} %multiply_add_fusion.2), channel_id=1, source_target_pairs={{16,0},{32,16},{48,32},{64,48},{80,64},{96,80},{112,96},{128,112},... | collective-permute-start | bytes 393224 | tf_op jit(solution)/shard_map/while/body/eval_jaxpr/ppermute | solution.py:10
  199.3 6.5 %collective-permute-start = (f32[4,64,128]{2,1,0:T(8,128)S(1)}, f32[4,64,128]{2,1,0:T(8,128)S(1)}, u32[]{:S(2)}, u32[]{:S(2)}) collective-permute-start(f32[4,64,128]{2,1,0:T(8,128)S(1)} %multiply_add_fusion.2), channel_id=1, source_target_pairs={{16,0},{32,16},{48,32},{64,48},{80,64},{96,80},{112,96},{128,112},... | collective-permute-start | bytes 393224 | tf_op jit(solution)/shard_map/while/body/eval_jaxpr/ppermute | solution.py:10
  208.4 6.5 %collective-permute-start = (f32[4,64,128]{2,1,0:T(8,128)S(1)}, f32[4,64,128]{2,1,0:T(8,128)S(1)}, u32[]{:S(2)}, u32[]{:S(2)}) collective-permute-start(f32[4,64,128]{2,1,0:T(8,128)S(1)} %multiply_add_fusion.2), channel_id=1, source_target_pairs={{16,0},{32,16},{48,32},{64,48},{80,64},{96,80},{112,96},{128,112},... | collective-permute-start | bytes 393224 | tf_op jit(solution)/shard_map/while/body/eval_jaxpr/ppermute | solution.py:10
  214.8 2.5 collective-permute-done
  217.4 6.5 %collective-permute-start = (f32[4,64,128]{2,1,0:T(8,128)S(1)}, f32[4,64,128]{2,1,0:T(8,128)S(1)}, u32[]{:S(2)}, u32[]{:S(2)}) collective-permute-start(f32[4,64,128]{2,1,0:T(8,128)S(1)} %multiply_add_fusion.2), channel_id=1, source_target_pairs={{16,0},{32,16},{48,32},{64,48},{80,64},{96,80},{112,96},{128,112},... | collective-permute-start | bytes 393224 | tf_op jit(solution)/shard_map/while/body/eval_jaxpr/ppermute | solution.py:10
  223.9 2.5 collective-permute-done
  226.5 6.5 %collective-permute-start = (f32[4,64,128]{2,1,0:T(8,128)S(1)}, f32[4,64,128]{2,1,0:T(8,128)S(1)}, u32[]{:S(2)}, u32[]{:S(2)}) collective-permute-start(f32[4,64,128]{2,1,0:T(8,128)S(1)} %multiply_add_fusion.2), channel_id=1, source_target_pairs={{16,0},{32,16},{48,32},{64,48},{80,64},{96,80},{112,96},{128,112},... | collective-permute-start | bytes 393224 | tf_op jit(solution)/shard_map/while/body/eval_jaxpr/ppermute | solution.py:10
  235.6 6.5 %collective-permute-start = (f32[4,64,128]{2,1,0:T(8,128)S(1)}, f32[4,64,128]{2,1,0:T(8,128)S(1)}, u32[]{:S(2)}, u32[]{:S(2)}) collective-permute-start(f32[4,64,128]{2,1,0:T(8,128)S(1)} %multiply_add_fusion.2), channel_id=1, source_target_pairs={{16,0},{32,16},{48,32},{64,48},{80,64},{96,80},{112,96},{128,112},... | collective-permute-start | bytes 393224 | tf_op jit(solution)/shard_map/while/body/eval_jaxpr/ppermute | solution.py:10
  244.6 6.5 %collective-permute-start = (f32[4,64,128]{2,1,0:T(8,128)S(1)}, f32[4,64,128]{2,1,0:T(8,128)S(1)}, u32[]{:S(2)}, u32[]{:S(2)}) collective-permute-start(f32[4,64,128]{2,1,0:T(8,128)S(1)} %multiply_add_fusion.2), channel_id=1, source_target_pairs={{16,0},{32,16},{48,32},{64,48},{80,64},{96,80},{112,96},{128,112},... | collective-permute-start | bytes 393224 | tf_op jit(solution)/shard_map/while/body/eval_jaxpr/ppermute | solution.py:10
  251.1 2.5 collective-permute-done
  253.7 6.5 %collective-permute-start = (f32[4,64,128]{2,1,0:T(8,128)S(1)}, f32[4,64,128]{2,1,0:T(8,128)S(1)}, u32[]{:S(2)}, u32[]{:S(2)}) collective-permute-start(f32[4,64,128]{2,1,0:T(8,128)S(1)} %multiply_add_fusion.2), channel_id=1, source_target_pairs={{16,0},{32,16},{48,32},{64,48},{80,64},{96,80},{112,96},{128,112},... | collective-permute-start | bytes 393224 | tf_op jit(solution)/shard_map/while/body/eval_jaxpr/ppermute | solution.py:10
  260.2 2.5 collective-permute-done
  262.8 6.5 %collective-permute-start = (f32[4,64,128]{2,1,0:T(8,128)S(1)}, f32[4,64,128]{2,1,0:T(8,128)S(1)}, u32[]{:S(2)}, u32[]{:S(2)}) collective-permute-start(f32[4,64,128]{2,1,0:T(8,128)S(1)} %multiply_add_fusion.2), channel_id=1, source_target_pairs={{16,0},{32,16},{48,32},{64,48},{80,64},{96,80},{112,96},{128,112},... | collective-permute-start | bytes 393224 | tf_op jit(solution)/shard_map/while/body/eval_jaxpr/ppermute | solution.py:10
  271.8 6.5 %collective-permute-start = (f32[4,64,128]{2,1,0:T(8,128)S(1)}, f32[4,64,128]{2,1,0:T(8,128)S(1)}, u32[]{:S(2)}, u32[]{:S(2)}) collective-permute-start(f32[4,64,128]{2,1,0:T(8,128)S(1)} %multiply_add_fusion.2), channel_id=1, source_target_pairs={{16,0},{32,16},{48,32},{64,48},{80,64},{96,80},{112,96},{128,112},... | collective-permute-start | bytes 393224 | tf_op jit(solution)/shard_map/while/body/eval_jaxpr/ppermute | solution.py:10
  280.9 6.5 %collective-permute-start = (f32[4,64,128]{2,1,0:T(8,128)S(1)}, f32[4,64,128]{2,1,0:T(8,128)S(1)}, u32[]{:S(2)}, u32[]{:S(2)}) collective-permute-start(f32[4,64,128]{2,1,0:T(8,128)S(1)} %multiply_add_fusion.2), channel_id=1, source_target_pairs={{16,0},{32,16},{48,32},{64,48},{80,64},{96,80},{112,96},{128,112},... | collective-permute-start | bytes 393224 | tf_op jit(solution)/shard_map/while/body/eval_jaxpr/ppermute | solution.py:10
  287.4 2.5 collective-permute-done
  290.0 6.5 %collective-permute-start = (f32[4,64,128]{2,1,0:T(8,128)S(1)}, f32[4,64,128]{2,1,0:T(8,128)S(1)}, u32[]{:S(2)}, u32[]{:S(2)}) collective-permute-start(f32[4,64,128]{2,1,0:T(8,128)S(1)} %multiply_add_fusion.2), channel_id=1, source_target_pairs={{16,0},{32,16},{48,32},{64,48},{80,64},{96,80},{112,96},{128,112},... | collective-permute-start | bytes 393224 | tf_op jit(solution)/shard_map/while/body/eval_jaxpr/ppermute | solution.py:10
  299.0 6.5 %collective-permute-start = (f32[4,64,128]{2,1,0:T(8,128)S(1)}, f32[4,64,128]{2,1,0:T(8,128)S(1)}, u32[]{:S(2)}, u32[]{:S(2)}) collective-permute-start(f32[4,64,128]{2,1,0:T(8,128)S(1)} %multiply_add_fusion.2), channel_id=1, source_target_pairs={{16,0},{32,16},{48,32},{64,48},{80,64},{96,80},{112,96},{128,112},... | collective-permute-start | bytes 393224 | tf_op jit(solution)/shard_map/while/body/eval_jaxpr/ppermute | solution.py:10
  308.1 6.5 %collective-permute-start = (f32[4,64,128]{2,1,0:T(8,128)S(1)}, f32[4,64,128]{2,1,0:T(8,128)S(1)}, u32[]{:S(2)}, u32[]{:S(2)}) collective-permute-start(f32[4,64,128]{2,1,0:T(8,128)S(1)} %multiply_add_fusion.2), channel_id=1, source_target_pairs={{16,0},{32,16},{48,32},{64,48},{80,64},{96,80},{112,96},{128,112},... | collective-permute-start | bytes 393224 | tf_op jit(solution)/shard_map/while/body/eval_jaxpr/ppermute | solution.py:10
  314.6 2.5 collective-permute-done
  317.2 6.5 %collective-permute-start = (f32[4,64,128]{2,1,0:T(8,128)S(1)}, f32[4,64,128]{2,1,0:T(8,128)S(1)}, u32[]{:S(2)}, u32[]{:S(2)}) collective-permute-start(f32[4,64,128]{2,1,0:T(8,128)S(1)} %multiply_add_fusion.2), channel_id=1, source_target_pairs={{16,0},{32,16},{48,32},{64,48},{80,64},{96,80},{112,96},{128,112},... | collective-permute-start | bytes 393224 | tf_op jit(solution)/shard_map/while/body/eval_jaxpr/ppermute | solution.py:10
  323.7 2.5 collective-permute-done
  326.2 6.5 %collective-permute-start = (f32[4,64,128]{2,1,0:T(8,128)S(1)}, f32[4,64,128]{2,1,0:T(8,128)S(1)}, u32[]{:S(2)}, u32[]{:S(2)}) collective-permute-start(f32[4,64,128]{2,1,0:T(8,128)S(1)} %multiply_add_fusion.2), channel_id=1, source_target_pairs={{16,0},{32,16},{48,32},{64,48},{80,64},{96,80},{112,96},{128,112},... | collective-permute-start | bytes 393224 | tf_op jit(solution)/shard_map/while/body/eval_jaxpr/ppermute | solution.py:10
  335.3 6.5 %collective-permute-start = (f32[4,64,128]{2,1,0:T(8,128)S(1)}, f32[4,64,128]{2,1,0:T(8,128)S(1)}, u32[]{:S(2)}, u32[]{:S(2)}) collective-permute-start(f32[4,64,128]{2,1,0:T(8,128)S(1)} %multiply_add_fusion.2), channel_id=1, source_target_pairs={{16,0},{32,16},{48,32},{64,48},{80,64},{96,80},{112,96},{128,112},... | collective-permute-start | bytes 393224 | tf_op jit(solution)/shard_map/while/body/eval_jaxpr/ppermute | solution.py:10
  344.4 6.5 %collective-permute-start = (f32[4,64,128]{2,1,0:T(8,128)S(1)}, f32[4,64,128]{2,1,0:T(8,128)S(1)}, u32[]{:S(2)}, u32[]{:S(2)}) collective-permute-start(f32[4,64,128]{2,1,0:T(8,128)S(1)} %multiply_add_fusion.2), channel_id=1, source_target_pairs={{16,0},{32,16},{48,32},{64,48},{80,64},{96,80},{112,96},{128,112},... | collective-permute-start | bytes 393224 | tf_op jit(solution)/shard_map/while/body/eval_jaxpr/ppermute | solution.py:10
  350.9 2.5 collective-permute-done
  353.4 6.5 %collective-permute-start = (f32[4,64,128]{2,1,0:T(8,128)S(1)}, f32[4,64,128]{2,1,0:T(8,128)S(1)}, u32[]{:S(2)}, u32[]{:S(2)}) collective-permute-start(f32[4,64,128]{2,1,0:T(8,128)S(1)} %multiply_add_fusion.2), channel_id=1, source_target_pairs={{16,0},{32,16},{48,32},{64,48},{80,64},{96,80},{112,96},{128,112},... | collective-permute-start | bytes 393224 | tf_op jit(solution)/shard_map/while/body/eval_jaxpr/ppermute | solution.py:10
  362.5 6.5 %collective-permute-start = (f32[4,64,128]{2,1,0:T(8,128)S(1)}, f32[4,64,128]{2,1,0:T(8,128)S(1)}, u32[]{:S(2)}, u32[]{:S(2)}) collective-permute-start(f32[4,64,128]{2,1,0:T(8,128)S(1)} %multiply_add_fusion.2), channel_id=1, source_target_pairs={{16,0},{32,16},{48,32},{64,48},{80,64},{96,80},{112,96},{128,112},... | collective-permute-start | bytes 393224 | tf_op jit(solution)/shard_map/while/body/eval_jaxpr/ppermute | solution.py:10
  371.6 6.5 %collective-permute-start = (f32[4,64,128]{2,1,0:T(8,128)S(1)}, f32[4,64,128]{2,1,0:T(8,128)S(1)}, u32[]{:S(2)}, u32[]{:S(2)}) collective-permute-start(f32[4,64,128]{2,1,0:T(8,128)S(1)} %multiply_add_fusion.2), channel_id=1, source_target_pairs={{16,0},{32,16},{48,32},{64,48},{80,64},{96,80},{112,96},{128,112},... | collective-permute-start | bytes 393224 | tf_op jit(solution)/shard_map/while/body/eval_jaxpr/ppermute | solution.py:10
  380.6 6.5 %collective-permute-start = (f32[4,64,128]{2,1,0:T(8,128)S(1)}, f32[4,64,128]{2,1,0:T(8,128)S(1)}, u32[]{:S(2)}, u32[]{:S(2)}) collective-permute-start(f32[4,64,128]{2,1,0:T(8,128)S(1)} %multiply_add_fusion.2), channel_id=1, source_target_pairs={{16,0},{32,16},{48,32},{64,48},{80,64},{96,80},{112,96},{128,112},... | collective-permute-start | bytes 393224 | tf_op jit(solution)/shard_map/while/body/eval_jaxpr/ppermute | solution.py:10
  389.7 6.5 %collective-permute-start = (f32[4,64,128]{2,1,0:T(8,128)S(1)}, f32[4,64,128]{2,1,0:T(8,128)S(1)}, u32[]{:S(2)}, u32[]{:S(2)}) collective-permute-start(f32[4,64,128]{2,1,0:T(8,128)S(1)} %multiply_add_fusion.2), channel_id=1, source_target_pairs={{16,0},{32,16},{48,32},{64,48},{80,64},{96,80},{112,96},{128,112},... | collective-permute-start | bytes 393224 | tf_op jit(solution)/shard_map/while/body/eval_jaxpr/ppermute | solution.py:10
  409.2 65.6 %psum.7 = f32[3,4]{1,0:T(4,128)S(1)} all-reduce(f32[3,4]{1,0:T(4,128)S(1)} %pad_maximum_fusion.1), channel_id=1, replica_groups=mesh['seq'=32,'head'=16] {'seq'}, use_global_device_ids=true, to_apply=%region_20.21 | all-reduce | flops 12 | bytes 96 | tf_op jit(solution)/shard_map/psum | solution.py:102
  475.4 49.7 %reduce-scatter.3.cloned.1.call-done = bf16[256,256]{0,1:T(8,128)(2,1)} async-done(((bf16[4096,256]{0,1:T(8,128)(2,1)}), bf16[256,256]{0,1:T(8,128)(2,1)}) %reduce-scatter.3.cloned.1.call-update) | async-done | bytes 131088 | tf_op jit(solution)/shard_map/reduce_scatter | solution.py:92
  526.7 109.5 %reduce-scatter.5.cloned.1.call-done = bf16[16,256]{1,0:T(8,128)(2,1)} async-done(((bf16[256,256]{1,0:T(8,128)(2,1)}), bf16[16,256]{1,0:T(8,128)(2,1)}) %reduce-scatter.5.cloned.1.call-update) | async-done | bytes 8208 | tf_op jit(solution)/shard_map/reduce_scatter | solution.py:100
  (123 shorter events, 72.7 us)
Async XLA Ops:
  7.2 392.8 %copy-start = (bf16[4096,256]{1,0:T(8,128)(2,1)S(1)}, bf16[4096,256]{1,0:T(8,128)(2,1)}, u32[]{:S(2)}) copy-start(bf16[4096,256]{1,0:T(8,128)(2,1)} %param.25) | copy-start | bytes 6291460
  7.2 110.5 %all-gather.2.cloned.1.call-start = ((), (), s32[]{:S(2)}) async-start(), calls=%async_computation.2 | async-start | bytes 2228224 | tf_op jit(solution)/shard_map/all_gather | solution.py:20
  7.9 517.1 %reduce-scatter.3.cloned.1.call-start = ((), (), s32[]{:S(2)}) async-start(), calls=%async_computation.3 | async-start | bytes 2228224 | tf_op jit(solution)/shard_map/reduce_scatter | solution.py:92
  117.7 3.1 copy-start.1
  120.9 277.8 %copy-start.3 = (bf16[256,128]{1,0:T(8,128)(2,1)S(1)}, bf16[256,128]{1,0:T(8,128)(2,1)}, u32[]{:S(2)}) copy-start(bf16[256,128]{1,0:T(8,128)(2,1)} %param.17) | copy-start | bytes 196612
  120.9 277.8 %copy-start.6 = (f32[4]{0:T(128)S(1)}, f32[4]{0:T(128)}, u32[]{:S(2)}) copy-start(f32[4]{0:T(128)} %param.22) | copy-start | bytes 52
  122.2 4.4 collective-permute-start
  126.7 9.0 %collective-permute-start = (f32[4,64,128]{2,1,0:T(8,128)S(1)}, f32[4,64,128]{2,1,0:T(8,128)S(1)}, u32[]{:S(2)}, u32[]{:S(2)}) collective-permute-start(f32[4,64,128]{2,1,0:T(8,128)S(1)} %multiply_add_fusion.2), channel_id=1, source_target_pairs={{16,0},{32,16},{48,32},{64,48},{80,64},{96,80},{112,96},{128,112},... | collective-permute-start | bytes 393224 | tf_op jit(solution)/shard_map/while/body/eval_jaxpr/ppermute | solution.py:10
  135.8 9.0 %collective-permute-start = (f32[4,64,128]{2,1,0:T(8,128)S(1)}, f32[4,64,128]{2,1,0:T(8,128)S(1)}, u32[]{:S(2)}, u32[]{:S(2)}) collective-permute-start(f32[4,64,128]{2,1,0:T(8,128)S(1)} %multiply_add_fusion.2), channel_id=1, source_target_pairs={{16,0},{32,16},{48,32},{64,48},{80,64},{96,80},{112,96},{128,112},... | collective-permute-start | bytes 393224 | tf_op jit(solution)/shard_map/while/body/eval_jaxpr/ppermute | solution.py:10
  144.9 9.0 %collective-permute-start = (f32[4,64,128]{2,1,0:T(8,128)S(1)}, f32[4,64,128]{2,1,0:T(8,128)S(1)}, u32[]{:S(2)}, u32[]{:S(2)}) collective-permute-start(f32[4,64,128]{2,1,0:T(8,128)S(1)} %multiply_add_fusion.2), channel_id=1, source_target_pairs={{16,0},{32,16},{48,32},{64,48},{80,64},{96,80},{112,96},{128,112},... | collective-permute-start | bytes 393224 | tf_op jit(solution)/shard_map/while/body/eval_jaxpr/ppermute | solution.py:10
  153.9 9.0 %collective-permute-start = (f32[4,64,128]{2,1,0:T(8,128)S(1)}, f32[4,64,128]{2,1,0:T(8,128)S(1)}, u32[]{:S(2)}, u32[]{:S(2)}) collective-permute-start(f32[4,64,128]{2,1,0:T(8,128)S(1)} %multiply_add_fusion.2), channel_id=1, source_target_pairs={{16,0},{32,16},{48,32},{64,48},{80,64},{96,80},{112,96},{128,112},... | collective-permute-start | bytes 393224 | tf_op jit(solution)/shard_map/while/body/eval_jaxpr/ppermute | solution.py:10
  163.0 9.0 %collective-permute-start = (f32[4,64,128]{2,1,0:T(8,128)S(1)}, f32[4,64,128]{2,1,0:T(8,128)S(1)}, u32[]{:S(2)}, u32[]{:S(2)}) collective-permute-start(f32[4,64,128]{2,1,0:T(8,128)S(1)} %multiply_add_fusion.2), channel_id=1, source_target_pairs={{16,0},{32,16},{48,32},{64,48},{80,64},{96,80},{112,96},{128,112},... | collective-permute-start | bytes 393224 | tf_op jit(solution)/shard_map/while/body/eval_jaxpr/ppermute | solution.py:10
  172.1 9.0 %collective-permute-start = (f32[4,64,128]{2,1,0:T(8,128)S(1)}, f32[4,64,128]{2,1,0:T(8,128)S(1)}, u32[]{:S(2)}, u32[]{:S(2)}) collective-permute-start(f32[4,64,128]{2,1,0:T(8,128)S(1)} %multiply_add_fusion.2), channel_id=1, source_target_pairs={{16,0},{32,16},{48,32},{64,48},{80,64},{96,80},{112,96},{128,112},... | collective-permute-start | bytes 393224 | tf_op jit(solution)/shard_map/while/body/eval_jaxpr/ppermute | solution.py:10
  181.1 9.0 %collective-permute-start = (f32[4,64,128]{2,1,0:T(8,128)S(1)}, f32[4,64,128]{2,1,0:T(8,128)S(1)}, u32[]{:S(2)}, u32[]{:S(2)}) collective-permute-start(f32[4,64,128]{2,1,0:T(8,128)S(1)} %multiply_add_fusion.2), channel_id=1, source_target_pairs={{16,0},{32,16},{48,32},{64,48},{80,64},{96,80},{112,96},{128,112},... | collective-permute-start | bytes 393224 | tf_op jit(solution)/shard_map/while/body/eval_jaxpr/ppermute | solution.py:10
  190.2 9.0 %collective-permute-start = (f32[4,64,128]{2,1,0:T(8,128)S(1)}, f32[4,64,128]{2,1,0:T(8,128)S(1)}, u32[]{:S(2)}, u32[]{:S(2)}) collective-permute-start(f32[4,64,128]{2,1,0:T(8,128)S(1)} %multiply_add_fusion.2), channel_id=1, source_target_pairs={{16,0},{32,16},{48,32},{64,48},{80,64},{96,80},{112,96},{128,112},... | collective-permute-start | bytes 393224 | tf_op jit(solution)/shard_map/while/body/eval_jaxpr/ppermute | solution.py:10
  199.3 9.0 %collective-permute-start = (f32[4,64,128]{2,1,0:T(8,128)S(1)}, f32[4,64,128]{2,1,0:T(8,128)S(1)}, u32[]{:S(2)}, u32[]{:S(2)}) collective-permute-start(f32[4,64,128]{2,1,0:T(8,128)S(1)} %multiply_add_fusion.2), channel_id=1, source_target_pairs={{16,0},{32,16},{48,32},{64,48},{80,64},{96,80},{112,96},{128,112},... | collective-permute-start | bytes 393224 | tf_op jit(solution)/shard_map/while/body/eval_jaxpr/ppermute | solution.py:10
  208.4 9.0 %collective-permute-start = (f32[4,64,128]{2,1,0:T(8,128)S(1)}, f32[4,64,128]{2,1,0:T(8,128)S(1)}, u32[]{:S(2)}, u32[]{:S(2)}) collective-permute-start(f32[4,64,128]{2,1,0:T(8,128)S(1)} %multiply_add_fusion.2), channel_id=1, source_target_pairs={{16,0},{32,16},{48,32},{64,48},{80,64},{96,80},{112,96},{128,112},... | collective-permute-start | bytes 393224 | tf_op jit(solution)/shard_map/while/body/eval_jaxpr/ppermute | solution.py:10
  217.4 9.0 %collective-permute-start = (f32[4,64,128]{2,1,0:T(8,128)S(1)}, f32[4,64,128]{2,1,0:T(8,128)S(1)}, u32[]{:S(2)}, u32[]{:S(2)}) collective-permute-start(f32[4,64,128]{2,1,0:T(8,128)S(1)} %multiply_add_fusion.2), channel_id=1, source_target_pairs={{16,0},{32,16},{48,32},{64,48},{80,64},{96,80},{112,96},{128,112},... | collective-permute-start | bytes 393224 | tf_op jit(solution)/shard_map/while/body/eval_jaxpr/ppermute | solution.py:10
  226.5 9.0 %collective-permute-start = (f32[4,64,128]{2,1,0:T(8,128)S(1)}, f32[4,64,128]{2,1,0:T(8,128)S(1)}, u32[]{:S(2)}, u32[]{:S(2)}) collective-permute-start(f32[4,64,128]{2,1,0:T(8,128)S(1)} %multiply_add_fusion.2), channel_id=1, source_target_pairs={{16,0},{32,16},{48,32},{64,48},{80,64},{96,80},{112,96},{128,112},... | collective-permute-start | bytes 393224 | tf_op jit(solution)/shard_map/while/body/eval_jaxpr/ppermute | solution.py:10
  235.6 9.0 %collective-permute-start = (f32[4,64,128]{2,1,0:T(8,128)S(1)}, f32[4,64,128]{2,1,0:T(8,128)S(1)}, u32[]{:S(2)}, u32[]{:S(2)}) collective-permute-start(f32[4,64,128]{2,1,0:T(8,128)S(1)} %multiply_add_fusion.2), channel_id=1, source_target_pairs={{16,0},{32,16},{48,32},{64,48},{80,64},{96,80},{112,96},{128,112},... | collective-permute-start | bytes 393224 | tf_op jit(solution)/shard_map/while/body/eval_jaxpr/ppermute | solution.py:10
  244.6 9.0 %collective-permute-start = (f32[4,64,128]{2,1,0:T(8,128)S(1)}, f32[4,64,128]{2,1,0:T(8,128)S(1)}, u32[]{:S(2)}, u32[]{:S(2)}) collective-permute-start(f32[4,64,128]{2,1,0:T(8,128)S(1)} %multiply_add_fusion.2), channel_id=1, source_target_pairs={{16,0},{32,16},{48,32},{64,48},{80,64},{96,80},{112,96},{128,112},... | collective-permute-start | bytes 393224 | tf_op jit(solution)/shard_map/while/body/eval_jaxpr/ppermute | solution.py:10
  253.7 9.0 %collective-permute-start = (f32[4,64,128]{2,1,0:T(8,128)S(1)}, f32[4,64,128]{2,1,0:T(8,128)S(1)}, u32[]{:S(2)}, u32[]{:S(2)}) collective-permute-start(f32[4,64,128]{2,1,0:T(8,128)S(1)} %multiply_add_fusion.2), channel_id=1, source_target_pairs={{16,0},{32,16},{48,32},{64,48},{80,64},{96,80},{112,96},{128,112},... | collective-permute-start | bytes 393224 | tf_op jit(solution)/shard_map/while/body/eval_jaxpr/ppermute | solution.py:10
  262.8 9.0 %collective-permute-start = (f32[4,64,128]{2,1,0:T(8,128)S(1)}, f32[4,64,128]{2,1,0:T(8,128)S(1)}, u32[]{:S(2)}, u32[]{:S(2)}) collective-permute-start(f32[4,64,128]{2,1,0:T(8,128)S(1)} %multiply_add_fusion.2), channel_id=1, source_target_pairs={{16,0},{32,16},{48,32},{64,48},{80,64},{96,80},{112,96},{128,112},... | collective-permute-start | bytes 393224 | tf_op jit(solution)/shard_map/while/body/eval_jaxpr/ppermute | solution.py:10
  271.8 9.0 %collective-permute-start = (f32[4,64,128]{2,1,0:T(8,128)S(1)}, f32[4,64,128]{2,1,0:T(8,128)S(1)}, u32[]{:S(2)}, u32[]{:S(2)}) collective-permute-start(f32[4,64,128]{2,1,0:T(8,128)S(1)} %multiply_add_fusion.2), channel_id=1, source_target_pairs={{16,0},{32,16},{48,32},{64,48},{80,64},{96,80},{112,96},{128,112},... | collective-permute-start | bytes 393224 | tf_op jit(solution)/shard_map/while/body/eval_jaxpr/ppermute | solution.py:10
  280.9 9.0 %collective-permute-start = (f32[4,64,128]{2,1,0:T(8,128)S(1)}, f32[4,64,128]{2,1,0:T(8,128)S(1)}, u32[]{:S(2)}, u32[]{:S(2)}) collective-permute-start(f32[4,64,128]{2,1,0:T(8,128)S(1)} %multiply_add_fusion.2), channel_id=1, source_target_pairs={{16,0},{32,16},{48,32},{64,48},{80,64},{96,80},{112,96},{128,112},... | collective-permute-start | bytes 393224 | tf_op jit(solution)/shard_map/while/body/eval_jaxpr/ppermute | solution.py:10
  290.0 9.0 %collective-permute-start = (f32[4,64,128]{2,1,0:T(8,128)S(1)}, f32[4,64,128]{2,1,0:T(8,128)S(1)}, u32[]{:S(2)}, u32[]{:S(2)}) collective-permute-start(f32[4,64,128]{2,1,0:T(8,128)S(1)} %multiply_add_fusion.2), channel_id=1, source_target_pairs={{16,0},{32,16},{48,32},{64,48},{80,64},{96,80},{112,96},{128,112},... | collective-permute-start | bytes 393224 | tf_op jit(solution)/shard_map/while/body/eval_jaxpr/ppermute | solution.py:10
  299.0 9.0 %collective-permute-start = (f32[4,64,128]{2,1,0:T(8,128)S(1)}, f32[4,64,128]{2,1,0:T(8,128)S(1)}, u32[]{:S(2)}, u32[]{:S(2)}) collective-permute-start(f32[4,64,128]{2,1,0:T(8,128)S(1)} %multiply_add_fusion.2), channel_id=1, source_target_pairs={{16,0},{32,16},{48,32},{64,48},{80,64},{96,80},{112,96},{128,112},... | collective-permute-start | bytes 393224 | tf_op jit(solution)/shard_map/while/body/eval_jaxpr/ppermute | solution.py:10
  308.1 9.0 %collective-permute-start = (f32[4,64,128]{2,1,0:T(8,128)S(1)}, f32[4,64,128]{2,1,0:T(8,128)S(1)}, u32[]{:S(2)}, u32[]{:S(2)}) collective-permute-start(f32[4,64,128]{2,1,0:T(8,128)S(1)} %multiply_add_fusion.2), channel_id=1, source_target_pairs={{16,0},{32,16},{48,32},{64,48},{80,64},{96,80},{112,96},{128,112},... | collective-permute-start | bytes 393224 | tf_op jit(solution)/shard_map/while/body/eval_jaxpr/ppermute | solution.py:10
  317.2 9.0 %collective-permute-start = (f32[4,64,128]{2,1,0:T(8,128)S(1)}, f32[4,64,128]{2,1,0:T(8,128)S(1)}, u32[]{:S(2)}, u32[]{:S(2)}) collective-permute-start(f32[4,64,128]{2,1,0:T(8,128)S(1)} %multiply_add_fusion.2), channel_id=1, source_target_pairs={{16,0},{32,16},{48,32},{64,48},{80,64},{96,80},{112,96},{128,112},... | collective-permute-start | bytes 393224 | tf_op jit(solution)/shard_map/while/body/eval_jaxpr/ppermute | solution.py:10
  326.2 9.0 %collective-permute-start = (f32[4,64,128]{2,1,0:T(8,128)S(1)}, f32[4,64,128]{2,1,0:T(8,128)S(1)}, u32[]{:S(2)}, u32[]{:S(2)}) collective-permute-start(f32[4,64,128]{2,1,0:T(8,128)S(1)} %multiply_add_fusion.2), channel_id=1, source_target_pairs={{16,0},{32,16},{48,32},{64,48},{80,64},{96,80},{112,96},{128,112},... | collective-permute-start | bytes 393224 | tf_op jit(solution)/shard_map/while/body/eval_jaxpr/ppermute | solution.py:10
  335.3 9.0 %collective-permute-start = (f32[4,64,128]{2,1,0:T(8,128)S(1)}, f32[4,64,128]{2,1,0:T(8,128)S(1)}, u32[]{:S(2)}, u32[]{:S(2)}) collective-permute-start(f32[4,64,128]{2,1,0:T(8,128)S(1)} %multiply_add_fusion.2), channel_id=1, source_target_pairs={{16,0},{32,16},{48,32},{64,48},{80,64},{96,80},{112,96},{128,112},... | collective-permute-start | bytes 393224 | tf_op jit(solution)/shard_map/while/body/eval_jaxpr/ppermute | solution.py:10
  344.4 9.0 %collective-permute-start = (f32[4,64,128]{2,1,0:T(8,128)S(1)}, f32[4,64,128]{2,1,0:T(8,128)S(1)}, u32[]{:S(2)}, u32[]{:S(2)}) collective-permute-start(f32[4,64,128]{2,1,0:T(8,128)S(1)} %multiply_add_fusion.2), channel_id=1, source_target_pairs={{16,0},{32,16},{48,32},{64,48},{80,64},{96,80},{112,96},{128,112},... | collective-permute-start | bytes 393224 | tf_op jit(solution)/shard_map/while/body/eval_jaxpr/ppermute | solution.py:10
  353.4 9.0 %collective-permute-start = (f32[4,64,128]{2,1,0:T(8,128)S(1)}, f32[4,64,128]{2,1,0:T(8,128)S(1)}, u32[]{:S(2)}, u32[]{:S(2)}) collective-permute-start(f32[4,64,128]{2,1,0:T(8,128)S(1)} %multiply_add_fusion.2), channel_id=1, source_target_pairs={{16,0},{32,16},{48,32},{64,48},{80,64},{96,80},{112,96},{128,112},... | collective-permute-start | bytes 393224 | tf_op jit(solution)/shard_map/while/body/eval_jaxpr/ppermute | solution.py:10
  362.5 9.0 %collective-permute-start = (f32[4,64,128]{2,1,0:T(8,128)S(1)}, f32[4,64,128]{2,1,0:T(8,128)S(1)}, u32[]{:S(2)}, u32[]{:S(2)}) collective-permute-start(f32[4,64,128]{2,1,0:T(8,128)S(1)} %multiply_add_fusion.2), channel_id=1, source_target_pairs={{16,0},{32,16},{48,32},{64,48},{80,64},{96,80},{112,96},{128,112},... | collective-permute-start | bytes 393224 | tf_op jit(solution)/shard_map/while/body/eval_jaxpr/ppermute | solution.py:10
  371.6 9.0 %collective-permute-start = (f32[4,64,128]{2,1,0:T(8,128)S(1)}, f32[4,64,128]{2,1,0:T(8,128)S(1)}, u32[]{:S(2)}, u32[]{:S(2)}) collective-permute-start(f32[4,64,128]{2,1,0:T(8,128)S(1)} %multiply_add_fusion.2), channel_id=1, source_target_pairs={{16,0},{32,16},{48,32},{64,48},{80,64},{96,80},{112,96},{128,112},... | collective-permute-start | bytes 393224 | tf_op jit(solution)/shard_map/while/body/eval_jaxpr/ppermute | solution.py:10
  380.6 9.0 %collective-permute-start = (f32[4,64,128]{2,1,0:T(8,128)S(1)}, f32[4,64,128]{2,1,0:T(8,128)S(1)}, u32[]{:S(2)}, u32[]{:S(2)}) collective-permute-start(f32[4,64,128]{2,1,0:T(8,128)S(1)} %multiply_add_fusion.2), channel_id=1, source_target_pairs={{16,0},{32,16},{48,32},{64,48},{80,64},{96,80},{112,96},{128,112},... | collective-permute-start | bytes 393224 | tf_op jit(solution)/shard_map/while/body/eval_jaxpr/ppermute | solution.py:10
  389.7 9.0 %collective-permute-start = (f32[4,64,128]{2,1,0:T(8,128)S(1)}, f32[4,64,128]{2,1,0:T(8,128)S(1)}, u32[]{:S(2)}, u32[]{:S(2)}) collective-permute-start(f32[4,64,128]{2,1,0:T(8,128)S(1)} %multiply_add_fusion.2), channel_id=1, source_target_pairs={{16,0},{32,16},{48,32},{64,48},{80,64},{96,80},{112,96},{128,112},... | collective-permute-start | bytes 393224 | tf_op jit(solution)/shard_map/while/body/eval_jaxpr/ppermute | solution.py:10
  402.1 0.8 copy-start.2
  402.1 1.7 copy-start.4
  402.1 1.7 copy-start.5
  402.1 234.1 %reduce-scatter.5.cloned.1.call-start = ((), (), s32[]{:S(2)}) async-start(), calls=%async_computation.4 | async-start | bytes 139264 | tf_op jit(solution)/shard_map/reduce_scatter | solution.py:100
Sparse Core Ops, SparseCore 0:
  11.0 106.6 all-gather.1
  402.2 122.7 reduce-scatter.2
  530.2 105.9 reduce-scatter.4
where the time goes:
time: 644 us; the launch traced here: 643 us
  waiting for transfers between devices  341 us (53%)
  starting transfers between devices  196 us (30%)
  blocking collectives  65.6 us (10%)
  between operations  13.9 us (2%)
  matrix products  10.6 us (2%)
  other arithmetic  9.97 us (2%)
    ppermute x31, starting transfers between devices, passed_along(): lax.ppermute(value, axis, [(source, source + steps) for source in range(i...  196 us
    reduce_scatter x1, waiting for transfers between devices, shards(): lax.psum_scatter(bc_part.astype(jnp.bfloat16), 'head', scatter_dimension=...  110 us
    all_gather x1, waiting for transfers between devices, shards(): lax.all_gather(out_grad, 'head', axis=1, tiled=True)  104 us
    ppermute x31, waiting for transfers between devices, passed_along(): lax.ppermute(value, axis, [(source, source + steps) for source in range(i...  77.4 us
    psum x1, blocking collectives, shards(): param_grad = lax.psum(param_terms, 'seq') * norm_scale  65.6 us
    reduce_scatter x1, waiting for transfers between devices, shards(): lax.psum_scatter(lax.dot_general(w_in, x_grad, contract_last, preferred_e...  49.7 us
  transfers between devices with their start and end apart: 34, of which 34 were waited for; matrix products, arithmetic and copies ran while one was open for 2% of the time, Pallas kernels for 0%

commit v1 on v0

--- a/solution.py
+++ b/solution.py
@@ -2,6 +2,11 @@
 import jax.numpy as jnp
 from jax import lax
 from jax.sharding import PartitionSpec as P
+
+
+def gather_and_add(array, name):
+    parts = lax.all_gather(array, name)
+    return jnp.sum(parts, axis=0)
 
 
 def passed_along(value, axis, steps):
@@ -99,7 +104,7 @@
     )
     bc_sum = lax.psum_scatter(bc_part.astype(jnp.bfloat16), "head", scatter_dimension=0, tiled=True)
     norm_scale = (lax.axis_size("seq") * tokens_here * head_dim) ** (-0.5)
-    param_grad = lax.psum(param_terms, "seq") * norm_scale
+    param_grad = gather_and_add(param_terms, "seq") * norm_scale
     return (in_part, bc_sum, dt_grad, param_grad)
 
 

time: 644 us -> 645 us (level)
  waiting for transfers between devices: 341 us -> 374 us
  blocking collectives: 65.6 us -> 33.6 us
    psum x1 -> x0, blocking collectives: 65.6 us -> none  [shards(): param_grad = lax.psum(param_terms, 'seq') * norm_scale]
    all_gather x0 -> x1, blocking collectives: none -> 33.6 us  [gather_and_add(): parts = lax.all_gather(array, name)]
    reduce_scatter x1, waiting for transfers between devices: 49.7 us -> 82.9 us  [shards(): lax.psum_scatter(lax.dot_general(w_in, x_grad, contract_last, preferred_e...]
where the time goes in v1:
time: 645 us; the launch traced here: 644 us
  waiting for transfers between devices  374 us (58%)
  starting transfers between devices  196 us (30%)
  blocking collectives  33.6 us (5%)
  between operations  13.9 us (2%)
  matrix products  10.6 us (2%)
  other arithmetic  10 us (2%)
    ppermute x31, starting transfers between devices, passed_along(): lax.ppermute(value, axis, [(source, source + steps) for source in range(i...  196 us
    reduce_scatter x1, waiting for transfers between devices, shards(): lax.psum_scatter(bc_part.astype(jnp.bfloat16), 'head', scatter_dimension=...  109 us
    all_gather x1, waiting for transfers between devices, shards(): lax.all_gather(out_grad, 'head', axis=1, tiled=True)  104 us
    reduce_scatter x1, waiting for transfers between devices, shards(): lax.psum_scatter(lax.dot_general(w_in, x_grad, contract_last, preferred_e...  82.9 us
    ppermute x31, waiting for transfers between devices, passed_along(): lax.ppermute(value, axis, [(source, source + steps) for source in range(i...  77.4 us
    all_gather x1, blocking collectives, gather_and_add(): parts = lax.all_gather(array, name)  33.6 us
  transfers between devices with their start and end apart: 34, of which 34 were waited for; matrix products, arithmetic and copies ran while one was open for 2% of the time, Pallas kernels for 0%

profile of v1, /device:TPU:2, one launch (start us, length us, event | category | flops | bytes accessed | tf_op | source)
XLA Modules:
  0.0 643.8 jit_solution(12040905796813344732)
XLA Ops:
  14.1 103.5 %all-gather.4.cloned.1.call-done = bf16[256,4096]{1,0:T(8,128)(2,1)} async-done(((bf16[256,256]{1,0:T(8,128)(2,1)}), bf16[256,4096]{1,0:T(8,128)(2,1)}) %all-gather.4.cloned.1.call-update) | async-done | bytes 2097168 | tf_op jit(solution)/shard_map/all_gather | solution.py:25
  117.7 3.1 fusion.14
  122.1 276.6 %while.11 = (s32[]{:T(128)}, f32[4,64,128]{2,1,0:T(8,128)S(1)}, f32[4]{0:T(128)S(1)}, f32[4,64,128]{2,1,0:T(8,128)S(1)}, s32[]{:T(128)}) while((s32[]{:T(128)}, f32[4,64,128]{2,1,0:T(8,128)S(1)}, f32[4]{0:T(128)S(1)}, f32[4,64,128]{2,1,0:T(8,128)S(1)}, s32[]{:T(128)}) %tuple.42), condition=%wide.region_3.4_spmd, body=%wide.region_2.3_spmd.sunk | while | flops 65538 | bytes 917621 | solution.py:65
  126.7 6.5 %collective-permute-start = (f32[4,64,128]{2,1,0:T(8,128)S(1)}, f32[4,64,128]{2,1,0:T(8,128)S(1)}, u32[]{:S(2)}, u32[]{:S(2)}) collective-permute-start(f32[4,64,128]{2,1,0:T(8,128)S(1)} %multiply_add_fusion.2), channel_id=1, source_target_pairs={{16,0},{32,16},{48,32},{64,48},{80,64},{96,80},{112,96},{128,112},... | collective-permute-start | bytes 393224 | tf_op jit(solution)/shard_map/while/body/eval_jaxpr/ppermute | solution.py:15
  135.8 6.5 %collective-permute-start = (f32[4,64,128]{2,1,0:T(8,128)S(1)}, f32[4,64,128]{2,1,0:T(8,128)S(1)}, u32[]{:S(2)}, u32[]{:S(2)}) collective-permute-start(f32[4,64,128]{2,1,0:T(8,128)S(1)} %multiply_add_fusion.2), channel_id=1, source_target_pairs={{16,0},{32,16},{48,32},{64,48},{80,64},{96,80},{112,96},{128,112},... | collective-permute-start | bytes 393224 | tf_op jit(solution)/shard_map/while/body/eval_jaxpr/ppermute | solution.py:15
  142.3 2.5 collective-permute-done
  144.9 6.5 %collective-permute-start = (f32[4,64,128]{2,1,0:T(8,128)S(1)}, f32[4,64,128]{2,1,0:T(8,128)S(1)}, u32[]{:S(2)}, u32[]{:S(2)}) collective-permute-start(f32[4,64,128]{2,1,0:T(8,128)S(1)} %multiply_add_fusion.2), channel_id=1, source_target_pairs={{16,0},{32,16},{48,32},{64,48},{80,64},{96,80},{112,96},{128,112},... | collective-permute-start | bytes 393224 | tf_op jit(solution)/shard_map/while/body/eval_jaxpr/ppermute | solution.py:15
  151.4 2.5 collective-permute-done
  153.9 6.5 %collective-permute-start = (f32[4,64,128]{2,1,0:T(8,128)S(1)}, f32[4,64,128]{2,1,0:T(8,128)S(1)}, u32[]{:S(2)}, u32[]{:S(2)}) collective-permute-start(f32[4,64,128]{2,1,0:T(8,128)S(1)} %multiply_add_fusion.2), channel_id=1, source_target_pairs={{16,0},{32,16},{48,32},{64,48},{80,64},{96,80},{112,96},{128,112},... | collective-permute-start | bytes 393224 | tf_op jit(solution)/shard_map/while/body/eval_jaxpr/ppermute | solution.py:15
  163.0 6.5 %collective-permute-start = (f32[4,64,128]{2,1,0:T(8,128)S(1)}, f32[4,64,128]{2,1,0:T(8,128)S(1)}, u32[]{:S(2)}, u32[]{:S(2)}) collective-permute-start(f32[4,64,128]{2,1,0:T(8,128)S(1)} %multiply_add_fusion.2), channel_id=1, source_target_pairs={{16,0},{32,16},{48,32},{64,48},{80,64},{96,80},{112,96},{128,112},... | collective-permute-start | bytes 393224 | tf_op jit(solution)/shard_map/while/body/eval_jaxpr/ppermute | solution.py:15
  172.1 6.5 %collective-permute-start = (f32[4,64,128]{2,1,0:T(8,128)S(1)}, f32[4,64,128]{2,1,0:T(8,128)S(1)}, u32[]{:S(2)}, u32[]{:S(2)}) collective-permute-start(f32[4,64,128]{2,1,0:T(8,128)S(1)} %multiply_add_fusion.2), channel_id=1, source_target_pairs={{16,0},{32,16},{48,32},{64,48},{80,64},{96,80},{112,96},{128,112},... | collective-permute-start | bytes 393224 | tf_op jit(solution)/shard_map/while/body/eval_jaxpr/ppermute | solution.py:15
  178.6 2.5 collective-permute-done
  181.1 6.5 %collective-permute-start = (f32[4,64,128]{2,1,0:T(8,128)S(1)}, f32[4,64,128]{2,1,0:T(8,128)S(1)}, u32[]{:S(2)}, u32[]{:S(2)}) collective-permute-start(f32[4,64,128]{2,1,0:T(8,128)S(1)} %multiply_add_fusion.2), channel_id=1, source_target_pairs={{16,0},{32,16},{48,32},{64,48},{80,64},{96,80},{112,96},{128,112},... | collective-permute-start | bytes 393224 | tf_op jit(solution)/shard_map/while/body/eval_jaxpr/ppermute | solution.py:15
  187.6 2.5 collective-permute-done
  190.2 6.5 %collective-permute-start = (f32[4,64,128]{2,1,0:T(8,128)S(1)}, f32[4,64,128]{2,1,0:T(8,128)S(1)}, u32[]{:S(2)}, u32[]{:S(2)}) collective-permute-start(f32[4,64,128]{2,1,0:T(8,128)S(1)} %multiply_add_fusion.2), channel_id=1, source_target_pairs={{16,0},{32,16},{48,32},{64,48},{80,64},{96,80},{112,96},{128,112},... | collective-permute-start | bytes 393224 | tf_op jit(solution)/shard_map/while/body/eval_jaxpr/ppermute | solution.py:15
  199.3 6.5 %collective-permute-start = (f32[4,64,128]{2,1,0:T(8,128)S(1)}, f32[4,64,128]{2,1,0:T(8,128)S(1)}, u32[]{:S(2)}, u32[]{:S(2)}) collective-permute-start(f32[4,64,128]{2,1,0:T(8,128)S(1)} %multiply_add_fusion.2), channel_id=1, source_target_pairs={{16,0},{32,16},{48,32},{64,48},{80,64},{96,80},{112,96},{128,112},... | collective-permute-start | bytes 393224 | tf_op jit(solution)/shard_map/while/body/eval_jaxpr/ppermute | solution.py:15
  208.4 6.5 %collective-permute-start = (f32[4,64,128]{2,1,0:T(8,128)S(1)}, f32[4,64,128]{2,1,0:T(8,128)S(1)}, u32[]{:S(2)}, u32[]{:S(2)}) collective-permute-start(f32[4,64,128]{2,1,0:T(8,128)S(1)} %multiply_add_fusion.2), channel_id=1, source_target_pairs={{16,0},{32,16},{48,32},{64,48},{80,64},{96,80},{112,96},{128,112},... | collective-permute-start | bytes 393224 | tf_op jit(solution)/shard_map/while/body/eval_jaxpr/ppermute | solution.py:15
  214.8 2.5 collective-permute-done
  217.4 6.5 %collective-permute-start = (f32[4,64,128]{2,1,0:T(8,128)S(1)}, f32[4,64,128]{2,1,0:T(8,128)S(1)}, u32[]{:S(2)}, u32[]{:S(2)}) collective-permute-start(f32[4,64,128]{2,1,0:T(8,128)S(1)} %multiply_add_fusion.2), channel_id=1, source_target_pairs={{16,0},{32,16},{48,32},{64,48},{80,64},{96,80},{112,96},{128,112},... | collective-permute-start | bytes 393224 | tf_op jit(solution)/shard_map/while/body/eval_jaxpr/ppermute | solution.py:15
  223.9 2.5 collective-permute-done
  226.5 6.5 %collective-permute-start = (f32[4,64,128]{2,1,0:T(8,128)S(1)}, f32[4,64,128]{2,1,0:T(8,128)S(1)}, u32[]{:S(2)}, u32[]{:S(2)}) collective-permute-start(f32[4,64,128]{2,1,0:T(8,128)S(1)} %multiply_add_fusion.2), channel_id=1, source_target_pairs={{16,0},{32,16},{48,32},{64,48},{80,64},{96,80},{112,96},{128,112},... | collective-permute-start | bytes 393224 | tf_op jit(solution)/shard_map/while/body/eval_jaxpr/ppermute | solution.py:15
  235.6 6.5 %collective-permute-start = (f32[4,64,128]{2,1,0:T(8,128)S(1)}, f32[4,64,128]{2,1,0:T(8,128)S(1)}, u32[]{:S(2)}, u32[]{:S(2)}) collective-permute-start(f32[4,64,128]{2,1,0:T(8,128)S(1)} %multiply_add_fusion.2), channel_id=1, source_target_pairs={{16,0},{32,16},{48,32},{64,48},{80,64},{96,80},{112,96},{128,112},... | collective-permute-start | bytes 393224 | tf_op jit(solution)/shard_map/while/body/eval_jaxpr/ppermute | solution.py:15
  244.6 6.5 %collective-permute-start = (f32[4,64,128]{2,1,0:T(8,128)S(1)}, f32[4,64,128]{2,1,0:T(8,128)S(1)}, u32[]{:S(2)}, u32[]{:S(2)}) collective-permute-start(f32[4,64,128]{2,1,0:T(8,128)S(1)} %multiply_add_fusion.2), channel_id=1, source_target_pairs={{16,0},{32,16},{48,32},{64,48},{80,64},{96,80},{112,96},{128,112},... | collective-permute-start | bytes 393224 | tf_op jit(solution)/shard_map/while/body/eval_jaxpr/ppermute | solution.py:15
  251.1 2.5 collective-permute-done
  253.7 6.5 %collective-permute-start = (f32[4,64,128]{2,1,0:T(8,128)S(1)}, f32[4,64,128]{2,1,0:T(8,128)S(1)}, u32[]{:S(2)}, u32[]{:S(2)}) collective-permute-start(f32[4,64,128]{2,1,0:T(8,128)S(1)} %multiply_add_fusion.2), channel_id=1, source_target_pairs={{16,0},{32,16},{48,32},{64,48},{80,64},{96,80},{112,96},{128,112},... | collective-permute-start | bytes 393224 | tf_op jit(solution)/shard_map/while/body/eval_jaxpr/ppermute | solution.py:15
  260.2 2.5 collective-permute-done
  262.8 6.5 %collective-permute-start = (f32[4,64,128]{2,1,0:T(8,128)S(1)}, f32[4,64,128]{2,1,0:T(8,128)S(1)}, u32[]{:S(2)}, u32[]{:S(2)}) collective-permute-start(f32[4,64,128]{2,1,0:T(8,128)S(1)} %multiply_add_fusion.2), channel_id=1, source_target_pairs={{16,0},{32,16},{48,32},{64,48},{80,64},{96,80},{112,96},{128,112},... | collective-permute-start | bytes 393224 | tf_op jit(solution)/shard_map/while/body/eval_jaxpr/ppermute | solution.py:15
  271.8 6.5 %collective-permute-start = (f32[4,64,128]{2,1,0:T(8,128)S(1)}, f32[4,64,128]{2,1,0:T(8,128)S(1)}, u32[]{:S(2)}, u32[]{:S(2)}) collective-permute-start(f32[4,64,128]{2,1,0:T(8,128)S(1)} %multiply_add_fusion.2), channel_id=1, source_target_pairs={{16,0},{32,16},{48,32},{64,48},{80,64},{96,80},{112,96},{128,112},... | collective-permute-start | bytes 393224 | tf_op jit(solution)/shard_map/while/body/eval_jaxpr/ppermute | solution.py:15
  280.9 6.5 %collective-permute-start = (f32[4,64,128]{2,1,0:T(8,128)S(1)}, f32[4,64,128]{2,1,0:T(8,128)S(1)}, u32[]{:S(2)}, u32[]{:S(2)}) collective-permute-start(f32[4,64,128]{2,1,0:T(8,128)S(1)} %multiply_add_fusion.2), channel_id=1, source_target_pairs={{16,0},{32,16},{48,32},{64,48},{80,64},{96,80},{112,96},{128,112},... | collective-permute-start | bytes 393224 | tf_op jit(solution)/shard_map/while/body/eval_jaxpr/ppermute | solution.py:15
  287.4 2.5 collective-permute-done
  290.0 6.5 %collective-permute-start = (f32[4,64,128]{2,1,0:T(8,128)S(1)}, f32[4,64,128]{2,1,0:T(8,128)S(1)}, u32[]{:S(2)}, u32[]{:S(2)}) collective-permute-start(f32[4,64,128]{2,1,0:T(8,128)S(1)} %multiply_add_fusion.2), channel_id=1, source_target_pairs={{16,0},{32,16},{48,32},{64,48},{80,64},{96,80},{112,96},{128,112},... | collective-permute-start | bytes 393224 | tf_op jit(solution)/shard_map/while/body/eval_jaxpr/ppermute | solution.py:15
  299.0 6.5 %collective-permute-start = (f32[4,64,128]{2,1,0:T(8,128)S(1)}, f32[4,64,128]{2,1,0:T(8,128)S(1)}, u32[]{:S(2)}, u32[]{:S(2)}) collective-permute-start(f32[4,64,128]{2,1,0:T(8,128)S(1)} %multiply_add_fusion.2), channel_id=1, source_target_pairs={{16,0},{32,16},{48,32},{64,48},{80,64},{96,80},{112,96},{128,112},... | collective-permute-start | bytes 393224 | tf_op jit(solution)/shard_map/while/body/eval_jaxpr/ppermute | solution.py:15
  308.1 6.5 %collective-permute-start = (f32[4,64,128]{2,1,0:T(8,128)S(1)}, f32[4,64,128]{2,1,0:T(8,128)S(1)}, u32[]{:S(2)}, u32[]{:S(2)}) collective-permute-start(f32[4,64,128]{2,1,0:T(8,128)S(1)} %multiply_add_fusion.2), channel_id=1, source_target_pairs={{16,0},{32,16},{48,32},{64,48},{80,64},{96,80},{112,96},{128,112},... | collective-permute-start | bytes 393224 | tf_op jit(solution)/shard_map/while/body/eval_jaxpr/ppermute | solution.py:15
  314.6 2.5 collective-permute-done
  317.2 6.5 %collective-permute-start = (f32[4,64,128]{2,1,0:T(8,128)S(1)}, f32[4,64,128]{2,1,0:T(8,128)S(1)}, u32[]{:S(2)}, u32[]{:S(2)}) collective-permute-start(f32[4,64,128]{2,1,0:T(8,128)S(1)} %multiply_add_fusion.2), channel_id=1, source_target_pairs={{16,0},{32,16},{48,32},{64,48},{80,64},{96,80},{112,96},{128,112},... | collective-permute-start | bytes 393224 | tf_op jit(solution)/shard_map/while/body/eval_jaxpr/ppermute | solution.py:15
  323.7 2.5 collective-permute-done
  326.2 6.5 %collective-permute-start = (f32[4,64,128]{2,1,0:T(8,128)S(1)}, f32[4,64,128]{2,1,0:T(8,128)S(1)}, u32[]{:S(2)}, u32[]{:S(2)}) collective-permute-start(f32[4,64,128]{2,1,0:T(8,128)S(1)} %multiply_add_fusion.2), channel_id=1, source_target_pairs={{16,0},{32,16},{48,32},{64,48},{80,64},{96,80},{112,96},{128,112},... | collective-permute-start | bytes 393224 | tf_op jit(solution)/shard_map/while/body/eval_jaxpr/ppermute | solution.py:15
  335.3 6.5 %collective-permute-start = (f32[4,64,128]{2,1,0:T(8,128)S(1)}, f32[4,64,128]{2,1,0:T(8,128)S(1)}, u32[]{:S(2)}, u32[]{:S(2)}) collective-permute-start(f32[4,64,128]{2,1,0:T(8,128)S(1)} %multiply_add_fusion.2), channel_id=1, source_target_pairs={{16,0},{32,16},{48,32},{64,48},{80,64},{96,80},{112,96},{128,112},... | collective-permute-start | bytes 393224 | tf_op jit(solution)/shard_map/while/body/eval_jaxpr/ppermute | solution.py:15
  344.4 6.5 %collective-permute-start = (f32[4,64,128]{2,1,0:T(8,128)S(1)}, f32[4,64,128]{2,1,0:T(8,128)S(1)}, u32[]{:S(2)}, u32[]{:S(2)}) collective-permute-start(f32[4,64,128]{2,1,0:T(8,128)S(1)} %multiply_add_fusion.2), channel_id=1, source_target_pairs={{16,0},{32,16},{48,32},{64,48},{80,64},{96,80},{112,96},{128,112},... | collective-permute-start | bytes 393224 | tf_op jit(solution)/shard_map/while/body/eval_jaxpr/ppermute | solution.py:15
  350.9 2.5 collective-permute-done
  353.4 6.5 %collective-permute-start = (f32[4,64,128]{2,1,0:T(8,128)S(1)}, f32[4,64,128]{2,1,0:T(8,128)S(1)}, u32[]{:S(2)}, u32[]{:S(2)}) collective-permute-start(f32[4,64,128]{2,1,0:T(8,128)S(1)} %multiply_add_fusion.2), channel_id=1, source_target_pairs={{16,0},{32,16},{48,32},{64,48},{80,64},{96,80},{112,96},{128,112},... | collective-permute-start | bytes 393224 | tf_op jit(solution)/shard_map/while/body/eval_jaxpr/ppermute | solution.py:15
  362.5 6.5 %collective-permute-start = (f32[4,64,128]{2,1,0:T(8,128)S(1)}, f32[4,64,128]{2,1,0:T(8,128)S(1)}, u32[]{:S(2)}, u32[]{:S(2)}) collective-permute-start(f32[4,64,128]{2,1,0:T(8,128)S(1)} %multiply_add_fusion.2), channel_id=1, source_target_pairs={{16,0},{32,16},{48,32},{64,48},{80,64},{96,80},{112,96},{128,112},... | collective-permute-start | bytes 393224 | tf_op jit(solution)/shard_map/while/body/eval_jaxpr/ppermute | solution.py:15
  371.6 6.5 %collective-permute-start = (f32[4,64,128]{2,1,0:T(8,128)S(1)}, f32[4,64,128]{2,1,0:T(8,128)S(1)}, u32[]{:S(2)}, u32[]{:S(2)}) collective-permute-start(f32[4,64,128]{2,1,0:T(8,128)S(1)} %multiply_add_fusion.2), channel_id=1, source_target_pairs={{16,0},{32,16},{48,32},{64,48},{80,64},{96,80},{112,96},{128,112},... | collective-permute-start | bytes 393224 | tf_op jit(solution)/shard_map/while/body/eval_jaxpr/ppermute | solution.py:15
  380.6 6.5 %collective-permute-start = (f32[4,64,128]{2,1,0:T(8,128)S(1)}, f32[4,64,128]{2,1,0:T(8,128)S(1)}, u32[]{:S(2)}, u32[]{:S(2)}) collective-permute-start(f32[4,64,128]{2,1,0:T(8,128)S(1)} %multiply_add_fusion.2), channel_id=1, source_target_pairs={{16,0},{32,16},{48,32},{64,48},{80,64},{96,80},{112,96},{128,112},... | collective-permute-start | bytes 393224 | tf_op jit(solution)/shard_map/while/body/eval_jaxpr/ppermute | solution.py:15
  389.7 6.5 %collective-permute-start = (f32[4,64,128]{2,1,0:T(8,128)S(1)}, f32[4,64,128]{2,1,0:T(8,128)S(1)}, u32[]{:S(2)}, u32[]{:S(2)}) collective-permute-start(f32[4,64,128]{2,1,0:T(8,128)S(1)} %multiply_add_fusion.2), channel_id=1, source_target_pairs={{16,0},{32,16},{48,32},{64,48},{80,64},{96,80},{112,96},{128,112},... | collective-permute-start | bytes 393224 | tf_op jit(solution)/shard_map/while/body/eval_jaxpr/ppermute | solution.py:15
  409.2 33.6 %all-gather.1 = f32[32,3,4]{2,1,0:T(4,128)S(1)} all-gather(f32[1,3,4]{2,1,0:T(4,128)S(1)} %maximum_bitcast_fusion), channel_id=2, replica_groups=mesh['seq'=32,'head'=16] {'seq'}, dimensions={0}, use_global_device_ids=true | all-gather | bytes 1584 | tf_op jit(solution)/shard_map/all_gather | solution.py:8
  443.4 82.9 %reduce-scatter.3.cloned.1.call-done = bf16[256,256]{0,1:T(8,128)(2,1)} async-done(((bf16[4096,256]{0,1:T(8,128)(2,1)}), bf16[256,256]{0,1:T(8,128)(2,1)}) %reduce-scatter.3.cloned.1.call-update) | async-done | bytes 131088 | tf_op jit(solution)/shard_map/reduce_scatter | solution.py:97
  527.9 109.4 %reduce-scatter.5.cloned.1.call-done = bf16[16,256]{1,0:T(8,128)(2,1)} async-done(((bf16[256,256]{1,0:T(8,128)(2,1)}), bf16[16,256]{1,0:T(8,128)(2,1)}) %reduce-scatter.5.cloned.1.call-update) | async-done | bytes 8208 | tf_op jit(solution)/shard_map/reduce_scatter | solution.py:105
  (124 shorter events, 72.7 us)
Async XLA Ops:
  7.2 392.8 %copy-start = (bf16[4096,256]{1,0:T(8,128)(2,1)S(1)}, bf16[4096,256]{1,0:T(8,128)(2,1)}, u32[]{:S(2)}) copy-start(bf16[4096,256]{1,0:T(8,128)(2,1)} %param.25) | copy-start | bytes 6291460
  7.2 110.5 %all-gather.4.cloned.1.call-start = ((), (), s32[]{:S(2)}) async-start(), calls=%async_computation.2 | async-start | bytes 2228224 | tf_op jit(solution)/shard_map/all_gather | solution.py:25
  7.9 518.3 %reduce-scatter.3.cloned.1.call-start = ((), (), s32[]{:S(2)}) async-start(), calls=%async_computation.3 | async-start | bytes 2228224 | tf_op jit(solution)/shard_map/reduce_scatter | solution.py:97
  117.7 3.1 copy-start.1
  120.9 277.8 %copy-start.3 = (bf16[256,128]{1,0:T(8,128)(2,1)S(1)}, bf16[256,128]{1,0:T(8,128)(2,1)}, u32[]{:S(2)}) copy-start(bf16[256,128]{1,0:T(8,128)(2,1)} %param.17) | copy-start | bytes 196612
  120.9 277.8 %copy-start.6 = (f32[4]{0:T(128)S(1)}, f32[4]{0:T(128)}, u32[]{:S(2)}) copy-start(f32[4]{0:T(128)} %param.22) | copy-start | bytes 52
  122.2 4.4 collective-permute-start
  126.7 9.0 %collective-permute-start = (f32[4,64,128]{2,1,0:T(8,128)S(1)}, f32[4,64,128]{2,1,0:T(8,128)S(1)}, u32[]{:S(2)}, u32[]{:S(2)}) collective-permute-start(f32[4,64,128]{2,1,0:T(8,128)S(1)} %multiply_add_fusion.2), channel_id=1, source_target_pairs={{16,0},{32,16},{48,32},{64,48},{80,64},{96,80},{112,96},{128,112},... | collective-permute-start | bytes 393224 | tf_op jit(solution)/shard_map/while/body/eval_jaxpr/ppermute | solution.py:15
  135.8 9.0 %collective-permute-start = (f32[4,64,128]{2,1,0:T(8,128)S(1)}, f32[4,64,128]{2,1,0:T(8,128)S(1)}, u32[]{:S(2)}, u32[]{:S(2)}) collective-permute-start(f32[4,64,128]{2,1,0:T(8,128)S(1)} %multiply_add_fusion.2), channel_id=1, source_target_pairs={{16,0},{32,16},{48,32},{64,48},{80,64},{96,80},{112,96},{128,112},... | collective-permute-start | bytes 393224 | tf_op jit(solution)/shard_map/while/body/eval_jaxpr/ppermute | solution.py:15
  144.9 9.0 %collective-permute-start = (f32[4,64,128]{2,1,0:T(8,128)S(1)}, f32[4,64,128]{2,1,0:T(8,128)S(1)}, u32[]{:S(2)}, u32[]{:S(2)}) collective-permute-start(f32[4,64,128]{2,1,0:T(8,128)S(1)} %multiply_add_fusion.2), channel_id=1, source_target_pairs={{16,0},{32,16},{48,32},{64,48},{80,64},{96,80},{112,96},{128,112},... | collective-permute-start | bytes 393224 | tf_op jit(solution)/shard_map/while/body/eval_jaxpr/ppermute | solution.py:15
  153.9 9.0 %collective-permute-start = (f32[4,64,128]{2,1,0:T(8,128)S(1)}, f32[4,64,128]{2,1,0:T(8,128)S(1)}, u32[]{:S(2)}, u32[]{:S(2)}) collective-permute-start(f32[4,64,128]{2,1,0:T(8,128)S(1)} %multiply_add_fusion.2), channel_id=1, source_target_pairs={{16,0},{32,16},{48,32},{64,48},{80,64},{96,80},{112,96},{128,112},... | collective-permute-start | bytes 393224 | tf_op jit(solution)/shard_map/while/body/eval_jaxpr/ppermute | solution.py:15
  163.0 9.0 %collective-permute-start = (f32[4,64,128]{2,1,0:T(8,128)S(1)}, f32[4,64,128]{2,1,0:T(8,128)S(1)}, u32[]{:S(2)}, u32[]{:S(2)}) collective-permute-start(f32[4,64,128]{2,1,0:T(8,128)S(1)} %multiply_add_fusion.2), channel_id=1, source_target_pairs={{16,0},{32,16},{48,32},{64,48},{80,64},{96,80},{112,96},{128,112},... | collective-permute-start | bytes 393224 | tf_op jit(solution)/shard_map/while/body/eval_jaxpr/ppermute | solution.py:15
  172.1 9.0 %collective-permute-start = (f32[4,64,128]{2,1,0:T(8,128)S(1)}, f32[4,64,128]{2,1,0:T(8,128)S(1)}, u32[]{:S(2)}, u32[]{:S(2)}) collective-permute-start(f32[4,64,128]{2,1,0:T(8,128)S(1)} %multiply_add_fusion.2), channel_id=1, source_target_pairs={{16,0},{32,16},{48,32},{64,48},{80,64},{96,80},{112,96},{128,112},... | collective-permute-start | bytes 393224 | tf_op jit(solution)/shard_map/while/body/eval_jaxpr/ppermute | solution.py:15
  181.1 9.0 %collective-permute-start = (f32[4,64,128]{2,1,0:T(8,128)S(1)}, f32[4,64,128]{2,1,0:T(8,128)S(1)}, u32[]{:S(2)}, u32[]{:S(2)}) collective-permute-start(f32[4,64,128]{2,1,0:T(8,128)S(1)} %multiply_add_fusion.2), channel_id=1, source_target_pairs={{16,0},{32,16},{48,32},{64,48},{80,64},{96,80},{112,96},{128,112},... | collective-permute-start | bytes 393224 | tf_op jit(solution)/shard_map/while/body/eval_jaxpr/ppermute | solution.py:15
  190.2 9.0 %collective-permute-start = (f32[4,64,128]{2,1,0:T(8,128)S(1)}, f32[4,64,128]{2,1,0:T(8,128)S(1)}, u32[]{:S(2)}, u32[]{:S(2)}) collective-permute-start(f32[4,64,128]{2,1,0:T(8,128)S(1)} %multiply_add_fusion.2), channel_id=1, source_target_pairs={{16,0},{32,16},{48,32},{64,48},{80,64},{96,80},{112,96},{128,112},... | collective-permute-start | bytes 393224 | tf_op jit(solution)/shard_map/while/body/eval_jaxpr/ppermute | solution.py:15
  199.3 9.0 %collective-permute-start = (f32[4,64,128]{2,1,0:T(8,128)S(1)}, f32[4,64,128]{2,1,0:T(8,128)S(1)}, u32[]{:S(2)}, u32[]{:S(2)}) collective-permute-start(f32[4,64,128]{2,1,0:T(8,128)S(1)} %multiply_add_fusion.2), channel_id=1, source_target_pairs={{16,0},{32,16},{48,32},{64,48},{80,64},{96,80},{112,96},{128,112},... | collective-permute-start | bytes 393224 | tf_op jit(solution)/shard_map/while/body/eval_jaxpr/ppermute | solution.py:15
  208.4 9.0 %collective-permute-start = (f32[4,64,128]{2,1,0:T(8,128)S(1)}, f32[4,64,128]{2,1,0:T(8,128)S(1)}, u32[]{:S(2)}, u32[]{:S(2)}) collective-permute-start(f32[4,64,128]{2,1,0:T(8,128)S(1)} %multiply_add_fusion.2), channel_id=1, source_target_pairs={{16,0},{32,16},{48,32},{64,48},{80,64},{96,80},{112,96},{128,112},... | collective-permute-start | bytes 393224 | tf_op jit(solution)/shard_map/while/body/eval_jaxpr/ppermute | solution.py:15
  217.4 9.0 %collective-permute-start = (f32[4,64,128]{2,1,0:T(8,128)S(1)}, f32[4,64,128]{2,1,0:T(8,128)S(1)}, u32[]{:S(2)}, u32[]{:S(2)}) collective-permute-start(f32[4,64,128]{2,1,0:T(8,128)S(1)} %multiply_add_fusion.2), channel_id=1, source_target_pairs={{16,0},{32,16},{48,32},{64,48},{80,64},{96,80},{112,96},{128,112},... | collective-permute-start | bytes 393224 | tf_op jit(solution)/shard_map/while/body/eval_jaxpr/ppermute | solution.py:15
  226.5 9.0 %collective-permute-start = (f32[4,64,128]{2,1,0:T(8,128)S(1)}, f32[4,64,128]{2,1,0:T(8,128)S(1)}, u32[]{:S(2)}, u32[]{:S(2)}) collective-permute-start(f32[4,64,128]{2,1,0:T(8,128)S(1)} %multiply_add_fusion.2), channel_id=1, source_target_pairs={{16,0},{32,16},{48,32},{64,48},{80,64},{96,80},{112,96},{128,112},... | collective-permute-start | bytes 393224 | tf_op jit(solution)/shard_map/while/body/eval_jaxpr/ppermute | solution.py:15
  235.6 9.0 %collective-permute-start = (f32[4,64,128]{2,1,0:T(8,128)S(1)}, f32[4,64,128]{2,1,0:T(8,128)S(1)}, u32[]{:S(2)}, u32[]{:S(2)}) collective-permute-start(f32[4,64,128]{2,1,0:T(8,128)S(1)} %multiply_add_fusion.2), channel_id=1, source_target_pairs={{16,0},{32,16},{48,32},{64,48},{80,64},{96,80},{112,96},{128,112},... | collective-permute-start | bytes 393224 | tf_op jit(solution)/shard_map/while/body/eval_jaxpr/ppermute | solution.py:15
  244.6 9.0 %collective-permute-start = (f32[4,64,128]{2,1,0:T(8,128)S(1)}, f32[4,64,128]{2,1,0:T(8,128)S(1)}, u32[]{:S(2)}, u32[]{:S(2)}) collective-permute-start(f32[4,64,128]{2,1,0:T(8,128)S(1)} %multiply_add_fusion.2), channel_id=1, source_target_pairs={{16,0},{32,16},{48,32},{64,48},{80,64},{96,80},{112,96},{128,112},... | collective-permute-start | bytes 393224 | tf_op jit(solution)/shard_map/while/body/eval_jaxpr/ppermute | solution.py:15
  253.7 9.0 %collective-permute-start = (f32[4,64,128]{2,1,0:T(8,128)S(1)}, f32[4,64,128]{2,1,0:T(8,128)S(1)}, u32[]{:S(2)}, u32[]{:S(2)}) collective-permute-start(f32[4,64,128]{2,1,0:T(8,128)S(1)} %multiply_add_fusion.2), channel_id=1, source_target_pairs={{16,0},{32,16},{48,32},{64,48},{80,64},{96,80},{112,96},{128,112},... | collective-permute-start | bytes 393224 | tf_op jit(solution)/shard_map/while/body/eval_jaxpr/ppermute | solution.py:15
  262.8 9.0 %collective-permute-start = (f32[4,64,128]{2,1,0:T(8,128)S(1)}, f32[4,64,128]{2,1,0:T(8,128)S(1)}, u32[]{:S(2)}, u32[]{:S(2)}) collective-permute-start(f32[4,64,128]{2,1,0:T(8,128)S(1)} %multiply_add_fusion.2), channel_id=1, source_target_pairs={{16,0},{32,16},{48,32},{64,48},{80,64},{96,80},{112,96},{128,112},... | collective-permute-start | bytes 393224 | tf_op jit(solution)/shard_map/while/body/eval_jaxpr/ppermute | solution.py:15
  271.8 9.0 %collective-permute-start = (f32[4,64,128]{2,1,0:T(8,128)S(1)}, f32[4,64,128]{2,1,0:T(8,128)S(1)}, u32[]{:S(2)}, u32[]{:S(2)}) collective-permute-start(f32[4,64,128]{2,1,0:T(8,128)S(1)} %multiply_add_fusion.2), channel_id=1, source_target_pairs={{16,0},{32,16},{48,32},{64,48},{80,64},{96,80},{112,96},{128,112},... | collective-permute-start | bytes 393224 | tf_op jit(solution)/shard_map/while/body/eval_jaxpr/ppermute | solution.py:15
  280.9 9.0 %collective-permute-start = (f32[4,64,128]{2,1,0:T(8,128)S(1)}, f32[4,64,128]{2,1,0:T(8,128)S(1)}, u32[]{:S(2)}, u32[]{:S(2)}) collective-permute-start(f32[4,64,128]{2,1,0:T(8,128)S(1)} %multiply_add_fusion.2), channel_id=1, source_target_pairs={{16,0},{32,16},{48,32},{64,48},{80,64},{96,80},{112,96},{128,112},... | collective-permute-start | bytes 393224 | tf_op jit(solution)/shard_map/while/body/eval_jaxpr/ppermute | solution.py:15
  290.0 9.0 %collective-permute-start = (f32[4,64,128]{2,1,0:T(8,128)S(1)}, f32[4,64,128]{2,1,0:T(8,128)S(1)}, u32[]{:S(2)}, u32[]{:S(2)}) collective-permute-start(f32[4,64,128]{2,1,0:T(8,128)S(1)} %multiply_add_fusion.2), channel_id=1, source_target_pairs={{16,0},{32,16},{48,32},{64,48},{80,64},{96,80},{112,96},{128,112},... | collective-permute-start | bytes 393224 | tf_op jit(solution)/shard_map/while/body/eval_jaxpr/ppermute | solution.py:15
  299.0 9.0 %collective-permute-start = (f32[4,64,128]{2,1,0:T(8,128)S(1)}, f32[4,64,128]{2,1,0:T(8,128)S(1)}, u32[]{:S(2)}, u32[]{:S(2)}) collective-permute-start(f32[4,64,128]{2,1,0:T(8,128)S(1)} %multiply_add_fusion.2), channel_id=1, source_target_pairs={{16,0},{32,16},{48,32},{64,48},{80,64},{96,80},{112,96},{128,112},... | collective-permute-start | bytes 393224 | tf_op jit(solution)/shard_map/while/body/eval_jaxpr/ppermute | solution.py:15
  308.1 9.0 %collective-permute-start = (f32[4,64,128]{2,1,0:T(8,128)S(1)}, f32[4,64,128]{2,1,0:T(8,128)S(1)}, u32[]{:S(2)}, u32[]{:S(2)}) collective-permute-start(f32[4,64,128]{2,1,0:T(8,128)S(1)} %multiply_add_fusion.2), channel_id=1, source_target_pairs={{16,0},{32,16},{48,32},{64,48},{80,64},{96,80},{112,96},{128,112},... | collective-permute-start | bytes 393224 | tf_op jit(solution)/shard_map/while/body/eval_jaxpr/ppermute | solution.py:15
  317.2 9.0 %collective-permute-start = (f32[4,64,128]{2,1,0:T(8,128)S(1)}, f32[4,64,128]{2,1,0:T(8,128)S(1)}, u32[]{:S(2)}, u32[]{:S(2)}) collective-permute-start(f32[4,64,128]{2,1,0:T(8,128)S(1)} %multiply_add_fusion.2), channel_id=1, source_target_pairs={{16,0},{32,16},{48,32},{64,48},{80,64},{96,80},{112,96},{128,112},... | collective-permute-start | bytes 393224 | tf_op jit(solution)/shard_map/while/body/eval_jaxpr/ppermute | solution.py:15
  326.2 9.0 %collective-permute-start = (f32[4,64,128]{2,1,0:T(8,128)S(1)}, f32[4,64,128]{2,1,0:T(8,128)S(1)}, u32[]{:S(2)}, u32[]{:S(2)}) collective-permute-start(f32[4,64,128]{2,1,0:T(8,128)S(1)} %multiply_add_fusion.2), channel_id=1, source_target_pairs={{16,0},{32,16},{48,32},{64,48},{80,64},{96,80},{112,96},{128,112},... | collective-permute-start | bytes 393224 | tf_op jit(solution)/shard_map/while/body/eval_jaxpr/ppermute | solution.py:15
  335.3 9.0 %collective-permute-start = (f32[4,64,128]{2,1,0:T(8,128)S(1)}, f32[4,64,128]{2,1,0:T(8,128)S(1)}, u32[]{:S(2)}, u32[]{:S(2)}) collective-permute-start(f32[4,64,128]{2,1,0:T(8,128)S(1)} %multiply_add_fusion.2), channel_id=1, source_target_pairs={{16,0},{32,16},{48,32},{64,48},{80,64},{96,80},{112,96},{128,112},... | collective-permute-start | bytes 393224 | tf_op jit(solution)/shard_map/while/body/eval_jaxpr/ppermute | solution.py:15
  344.4 9.0 %collective-permute-start = (f32[4,64,128]{2,1,0:T(8,128)S(1)}, f32[4,64,128]{2,1,0:T(8,128)S(1)}, u32[]{:S(2)}, u32[]{:S(2)}) collective-permute-start(f32[4,64,128]{2,1,0:T(8,128)S(1)} %multiply_add_fusion.2), channel_id=1, source_target_pairs={{16,0},{32,16},{48,32},{64,48},{80,64},{96,80},{112,96},{128,112},... | collective-permute-start | bytes 393224 | tf_op jit(solution)/shard_map/while/body/eval_jaxpr/ppermute | solution.py:15
  353.4 9.0 %collective-permute-start = (f32[4,64,128]{2,1,0:T(8,128)S(1)}, f32[4,64,128]{2,1,0:T(8,128)S(1)}, u32[]{:S(2)}, u32[]{:S(2)}) collective-permute-start(f32[4,64,128]{2,1,0:T(8,128)S(1)} %multiply_add_fusion.2), channel_id=1, source_target_pairs={{16,0},{32,16},{48,32},{64,48},{80,64},{96,80},{112,96},{128,112},... | collective-permute-start | bytes 393224 | tf_op jit(solution)/shard_map/while/body/eval_jaxpr/ppermute | solution.py:15
  362.5 9.0 %collective-permute-start = (f32[4,64,128]{2,1,0:T(8,128)S(1)}, f32[4,64,128]{2,1,0:T(8,128)S(1)}, u32[]{:S(2)}, u32[]{:S(2)}) collective-permute-start(f32[4,64,128]{2,1,0:T(8,128)S(1)} %multiply_add_fusion.2), channel_id=1, source_target_pairs={{16,0},{32,16},{48,32},{64,48},{80,64},{96,80},{112,96},{128,112},... | collective-permute-start | bytes 393224 | tf_op jit(solution)/shard_map/while/body/eval_jaxpr/ppermute | solution.py:15
  371.6 9.0 %collective-permute-start = (f32[4,64,128]{2,1,0:T(8,128)S(1)}, f32[4,64,128]{2,1,0:T(8,128)S(1)}, u32[]{:S(2)}, u32[]{:S(2)}) collective-permute-start(f32[4,64,128]{2,1,0:T(8,128)S(1)} %multiply_add_fusion.2), channel_id=1, source_target_pairs={{16,0},{32,16},{48,32},{64,48},{80,64},{96,80},{112,96},{128,112},... | collective-permute-start | bytes 393224 | tf_op jit(solution)/shard_map/while/body/eval_jaxpr/ppermute | solution.py:15
  380.6 9.0 %collective-permute-start = (f32[4,64,128]{2,1,0:T(8,128)S(1)}, f32[4,64,128]{2,1,0:T(8,128)S(1)}, u32[]{:S(2)}, u32[]{:S(2)}) collective-permute-start(f32[4,64,128]{2,1,0:T(8,128)S(1)} %multiply_add_fusion.2), channel_id=1, source_target_pairs={{16,0},{32,16},{48,32},{64,48},{80,64},{96,80},{112,96},{128,112},... | collective-permute-start | bytes 393224 | tf_op jit(solution)/shard_map/while/body/eval_jaxpr/ppermute | solution.py:15
  389.7 9.0 %collective-permute-start = (f32[4,64,128]{2,1,0:T(8,128)S(1)}, f32[4,64,128]{2,1,0:T(8,128)S(1)}, u32[]{:S(2)}, u32[]{:S(2)}) collective-permute-start(f32[4,64,128]{2,1,0:T(8,128)S(1)} %multiply_add_fusion.2), channel_id=1, source_target_pairs={{16,0},{32,16},{48,32},{64,48},{80,64},{96,80},{112,96},{128,112},... | collective-permute-start | bytes 393224 | tf_op jit(solution)/shard_map/while/body/eval_jaxpr/ppermute | solution.py:15
  402.1 0.8 copy-start.2
  402.1 1.7 copy-start.4
  402.1 1.7 copy-start.5
  402.1 235.2 %reduce-scatter.5.cloned.1.call-start = ((), (), s32[]{:S(2)}) async-start(), calls=%async_computation.4 | async-start | bytes 139264 | tf_op jit(solution)/shard_map/reduce_scatter | solution.py:105
Sparse Core Ops, SparseCore 0:
  11.0 106.6 all-gather.3
  402.2 123.9 reduce-scatter.2
  531.4 105.8 reduce-scatter.4
